TPU v7x, 128 devices: a whole 4x4x4 slice. The times are simulated.
128 devices in a mesh: row: 16 (over y_hi, x, core), col: 8 (over y_lo, z).
Axes of the slice: x: 4, y: 4 (y_hi: 2, y_lo: 2; y = y_hi * 2 + y_lo), z: 4, core: 2. Of those that a mesh axis runs over, the one named last changes fastest.
Arguments:
- blocks: float32 [4096, 24, 4096], P('row', 'col')
- columns: int32 [4096, 24], P('row', 'col'), may hold values from 0 to 4095, as said below
- counts: int32 [4096, 8], P('row', 'col'), may hold values from 0 to 3, as said below
- old_basis: float32 [128, 262144], P(None, 'row')
- vectors: float32 [16, 262144], P(None, 'row')
Outputs:
- new_block: float32 [16, 262144], P(None, 'row')
- coeffs: float32 [128, 16], replicated
- factor: float32 [16, 16], replicated
Inputs may be any that keep to these rules, and one draw needn't show every extreme that they name: `columns`: slot k * 3 + s of a block row names a global block column g held by column group k, that is (g % 256) // (256 / the number of column groups) == k; slot 0 of the group holding the row's own block column names that column. The counts of one block row sum to 11; the group holding the row's own block column has 3.
All inputs are finite; a program needn't handle non-finite values.
Results may differ from a plain program's by a relative error of at most 0.0003.
Values sent between devices are 32-bit elements; how exact they have to be, the bound alone decides.
A program may use at most 192 MiB of HBM per device.

v0:
```python
import jax
import jax.numpy as jnp
from jax import lax
from jax.sharding import PartitionSpec as P

B = 64
S = 16
SLOT = 3


def reduce_small(terms):
    return lax.psum(terms, "row")


def project(left, right):
    return jnp.dot(
        left, right.T, precision=lax.Precision.HIGHEST, preferred_element_type=jnp.float32
    )


def remove(target, coef_block, local_basis):
    return target - jnp.dot(coef_block.T, local_basis, precision=lax.Precision.HIGHEST)


def body(blocks, columns, counts, old_basis, vectors):
    row_count = lax.axis_size("row")
    col_count = lax.axis_size("col")
    rows_dev = counts.shape[0]
    sub_width = rows_dev // col_count
    col_index = lax.axis_index("col")
    mine = lax.dynamic_slice_in_dim(vectors, col_index * sub_width * B, sub_width * B, 1)
    pieces = lax.all_gather(mine, "row", axis=1, tiled=True)
    vector_grid = pieces.reshape(S, row_count * sub_width, B)
    within = columns % rows_dev
    local_ids = columns // rows_dev * sub_width + within % sub_width
    taken = jnp.take(vector_grid, local_ids, axis=1)
    live_mask = (jnp.arange(SLOT, dtype=jnp.int32)[None, :] < counts).astype(jnp.float32)
    block_mats = blocks.reshape(rows_dev, SLOT, B, B)
    partial_rows = jnp.einsum(
        "nrsb,rsba->nra",
        taken * live_mask[None, :, :, None],
        block_mats,
        precision=lax.Precision.HIGHEST,
    ).reshape(S, rows_dev * B)
    scale = 1.0 / float(old_basis.shape[1] * row_count)
    product = lax.psum(partial_rows, "col")
    first_proj = reduce_small(project(old_basis, product)) * scale
    once = remove(product, first_proj, old_basis)
    second_proj = reduce_small(project(old_basis, once)) * scale
    twice = remove(once, second_proj, old_basis)
    gram = reduce_small(project(twice, twice)) * scale
    factor = jnp.linalg.cholesky(gram)
    new_block = lax.linalg.triangular_solve(factor, twice, left_side=True, lower=True)
    return (new_block, first_proj + second_proj, factor)


def solution(mesh):
    return jax.shard_map(
        body,
        mesh=mesh,
        in_specs=(
            P("row", "col", None),
            P("row", "col"),
            P("row", "col"),
            P(None, "row"),
            P(None, "row"),
        ),
        out_specs=(P(None, "row"), P(), P()),
        check_vma=False,
    )
```

profile of v0, /device:TPU:1, one launch (start us, length us, event | category | flops | bytes accessed | tf_op | source)
XLA Modules:
  0.0 332.4 jit_solution(8025639032096762821)
XLA Ops:
  7.2 0.0 copy-start
  7.2 0.0 all-gather.2.cloned.1.call-start
  7.2 1.2 copy-done
  8.4 0.7 constant_dynamic-slice_fusion
  9.1 0.0 all-gather.2.cloned.1.call-update
  9.1 0.0 all-reduce.2.cloned.1.call-start
  9.1 12.6 %copy.16 = f32[256,3,4096]{0,2,1:T(8,128)} copy(f32[256,3,4096]{2,0,1:T(8,128)} %param.5) | data formatting | bytes 25165824 | tf_op args[0]
  21.8 0.0 copy-start.3
  21.8 0.0 copy-start.4
  21.8 23.5 %copy.17 = f32[256,3,64,64]{3,2,1,0:T(8,128)} copy(f32[256,3,64,64]{0,3,2,1:T(8,128)} %bitcast.37) | data formatting | bytes 25165824 | tf_op jit(solution)/shard_map/reshape | solution.py:38
  45.2 0.0 copy-done.3
  45.3 0.1 copy.14
  45.4 0.2 reshape.58
  45.6 0.2 copy.13
  45.8 0.0 copy-done.4
  45.8 0.1 fusion.10
  45.9 17.2 %all-gather.2.cloned.1.call-done = f32[16,32768]{1,0:T(8,128)} async-done(((f32[16,2048]{1,0:T(8,128)}), f32[16,32768]{1,0:T(8,128)}) %all-gather.2.cloned.1.call-update) | async-done | bytes 2097168 | tf_op jit(solution)/shard_map/all_gather | solution.py:32
  63.1 4.2 %reshape.53 = f32[16,512,64]{2,1,0:T(8,128)} reshape(f32[16,32768]{1,0:T(8,128)} %all-gather.2.cloned.1.call-done) | data formatting | bytes 4194304 | tf_op jit(solution)/shard_map/reshape | solution.py:33
  67.3 6.6 %copy.15 = f32[16,512,64]{2,0,1:T(8,128)} copy(f32[16,512,64]{2,1,0:T(8,128)} %reshape.53) | data formatting | bytes 4194304 | tf_op jit(solution)/shard_map/reshape | solution.py:33
  73.9 6.1 %gather_fusion = f32[768,16,64]{2,1,0:T(8,128)} fusion(f32[16,512,64]{2,0,1:T(8,128)} %copy.15, s32[1024]{0:T(1024)S(1)} %pad_clamp_fusion), kind=kCustom, calls=%fused_computation | custom fusion | bytes 6294528 | tf_op jit(solution)/shard_map/jit(_take)/gather | solution.py:36
  80.0 26.4 %fusion.7 = f32[16,256,64]{2,0,1:T(8,128)S(1)} fusion(f32[256,3,64,64]{3,2,1,0:T(8,128)} %copy.17, f32[256,3,16,64]{3,2,1,0:T(8,128)} %bitcast.36, f32[256,3]{1,0:T(8,128)S(1)} %fusion.10, pred[256,3]{1,0:T(8,128)(4,1)S(1)} %copy.13), kind=kOutput, calls=%fused_computation.10 | convolution fusion | flops 605552640 | bytes 16781056 | tf_op jit(solution)/shard_map/nrsb,rsba->nra/dot_general | solution.py:39
  106.4 0.7 copy.18
  107.1 1.6 reshape.55
  108.7 0.0 all-reduce.2.cloned.1.call-update
  108.7 70.8 %all-reduce.2.cloned.1.call-done = f32[16,16384]{1,0:T(8,128)} async-done(((f32[16,16384]{1,0:T(8,128)}), f32[16,16384]{1,0:T(8,128)}) %all-reduce.2.cloned.1.call-update) | async-done | bytes 1048592 | tf_op jit(solution)/shard_map/psum | solution.py:46
  179.6 0.0 copy-start.2
  179.6 9.1 %convolution_bitcast_fusion.1 = f32[128,16]{0,1:T(8,128)S(1)} fusion(f32[16,16384]{1,0:T(8,128)} %all-reduce.2.cloned.1.call-done, f32[128,16384]{1,0:T(8,128)} %param.8), kind=kOutput, calls=%fused_computation.12 | convolution fusion | flops 402653184 | bytes 9445376 | tf_op jit(solution)/shard_map/dot_general | solution.py:16
  188.7 38.7 %psum.29 = f32[128,16]{0,1:T(8,128)S(1)} all-reduce(f32[128,16]{0,1:T(8,128)S(1)} %convolution_bitcast_fusion.1), channel_id=1, replica_groups=mesh['row'=16,'col'=8] {'row'}, use_global_device_ids=true, to_apply=%region_1.2 | all-reduce | flops 2048 | bytes 16384 | tf_op jit(solution)/shard_map/psum | solution.py:12
  227.4 0.0 copy-done.2
  227.4 6.4 %convolution_subtract_fusion.1 = f32[16,16384]{1,0:T(8,128)S(1)} fusion(f32[16,16384]{1,0:T(8,128)S(1)} %copy-done.2, f32[128,16384]{1,0:T(8,128)} %param.8, f32[128,16]{0,1:T(8,128)S(1)} %psum.29), kind=kOutput, calls=%fused_computation.2 | convolution fusion | flops 402917376 | bytes 10493952 | tf_op jit(solution)/shard_map/dot_general | solution.py:22
  233.8 0.0 copy-start.1
  233.8 9.0 %convolution_bitcast_fusion = f32[128,16]{0,1:T(8,128)S(1)} fusion(f32[16,16384]{1,0:T(8,128)S(1)} %convolution_subtract_fusion.1, f32[128,16384]{1,0:T(8,128)} %param.8), kind=kOutput, calls=%fused_computation.11 | convolution fusion | flops 402653184 | bytes 9445376 | tf_op jit(solution)/shard_map/dot_general | solution.py:16
  242.8 33.7 %psum.30 = f32[128,16]{0,1:T(8,128)S(1)} all-reduce(f32[128,16]{0,1:T(8,128)S(1)} %convolution_bitcast_fusion), channel_id=1, replica_groups=mesh['row'=16,'col'=8] {'row'}, use_global_device_ids=true, to_apply=%region_2.3 | all-reduce | flops 2048 | bytes 16384 | tf_op jit(solution)/shard_map/psum | solution.py:12
  276.5 6.6 %convolution_subtract_fusion = f32[16,16384]{1,0:T(8,128)S(1)} fusion(f32[16,16384]{1,0:T(8,128)S(1)} %convolution_subtract_fusion.1, f32[128,16384]{1,0:T(8,128)} %param.8, f32[128,16]{0,1:T(8,128)S(1)} %psum.30), kind=kOutput, calls=%fused_computation.1 | convolution fusion | flops 402917376 | bytes 10493952 | tf_op jit(solution)/shard_map/dot_general | solution.py:22
  283.1 0.6 multiply_add_fusion
  283.7 1.5 fusion.26
  285.2 33.7 %psum.31 = f32[16,16]{0,1:T(8,128)S(1)} all-reduce(f32[16,16]{0,1:T(8,128)S(1)} %fusion.26), channel_id=1, replica_groups=mesh['row'=16,'col'=8] {'row'}, use_global_device_ids=true, to_apply=%region_3.4 | all-reduce | flops 256 | bytes 2048 | tf_op jit(solution)/shard_map/psum | solution.py:12
  318.8 0.1 copy.20
  318.9 1.5 cholesky.16
  320.4 0.6 compare_reduce_fusion
  321.1 1.2 select_bitcast_fusion
  322.3 1.2 custom-call.6
  323.5 2.0 fusion.11
  325.6 0.0 copy-done.1
  (5 shorter events, 0.1 us)
Async XLA Ops:
  7.2 1.2 copy-start
  7.2 55.9 %all-gather.2.cloned.1.call-start = ((), (), s32[]{:S(2)}) async-start(), calls=%async_computation | async-start | bytes 2228224 | tf_op jit(solution)/shard_map/all_gather | solution.py:32
  9.1 170.5 %all-reduce.2.cloned.1.call-start = ((), (), s32[]{:S(2)}) async-start(), calls=%async_computation.1 | async-start | bytes 2097152 | tf_op jit(solution)/shard_map/psum | solution.py:46
  21.8 23.5 %copy-start.3 = (s32[256,3]{0,1:T(4,128)S(1)}, s32[256,3]{0,1:T(4,128)}, u32[]{:S(2)}) copy-start(s32[256,3]{0,1:T(4,128)} %param.6) | copy-start | bytes 9220
  21.8 24.1 %copy-start.4 = (s32[256,1]{0,1:T(1,128)S(1)}, s32[256,1]{0,1:T(1,128)}, u32[]{:S(2)}) copy-start(s32[256,1]{0,1:T(1,128)} %param.7) | copy-start | bytes 3076
  179.6 47.9 %copy-start.2 = (f32[16,16384]{1,0:T(8,128)S(1)}, f32[16,16384]{1,0:T(8,128)}, u32[]{:S(2)}) copy-start(f32[16,16384]{1,0:T(8,128)} %all-reduce.2.cloned.1.call-done) | copy-start | bytes 3145732
  233.8 91.7 %copy-start.1 = (f32[16,16384]{1,0:T(8,128)S(1)}, f32[16,16384]{1,0:T(8,128)}, u32[]{:S(2)}) copy-start(f32[16,16384]{1,0:T(8,128)} %param.9) | copy-start | bytes 3145732
Sparse Core Ops, SparseCore 0:
  11.1 51.9 all-gather.1
  108.8 70.6 all-reduce.1
where the time goes:
time: 333 us; the launch traced here: 332 us
  blocking collectives  106 us (32%)
  waiting for transfers between devices  88 us (26%)
  matrix products  61 us (18%)
  local copies, waits for them, and re-layouts  57.7 us (17%)
  between operations  14.2 us (4%)
  other arithmetic  5.35 us (2%)
    psum x3, blocking collectives, reduce_small(): return lax.psum(terms, 'row')  106 us
    psum x1, waiting for transfers between devices, body(): product = lax.psum(partial_rows, 'col')  70.8 us
    dot_general x1, matrix products, body(): jnp.einsum('nrsb,rsba->nra', taken * live_mask[None, :, :, None], block_m...  26.4 us
    reshape x1, local copies, waits for them, and re-layouts, body(): block_mats = blocks.reshape(rows_dev, SLOT, B, B)  23.5 us
    dot_general x3, matrix products, project(): jnp.dot(left, right.T, precision=lax.Precision.HIGHEST, preferred_element...  19.6 us
    all_gather x1, waiting for transfers between devices, body(): pieces = lax.all_gather(mine, 'row', axis=1, tiled=True)  17.2 us
    unnamed x11, local copies, waits for them, and re-layouts  13.8 us
    dot_general x2, matrix products, remove(): jnp.dot(coef_block.T, local_basis, precision=lax.Precision.HIGHEST)  12.9 us
  transfers between devices with their start and end apart: 2, of which 2 were waited for; matrix products, arithmetic and copies ran while one was open for 11% of the time, Pallas kernels for 0%

commit v1 on v0

v1 whole, which is shorter than its diff:
```python
import functools

import jax
import jax.numpy as jnp
from jax import lax
from jax.experimental import pallas as pl
from jax.experimental.pallas import tpu as pltpu
from jax.sharding import PartitionSpec as P

f32 = jnp.float32
bf16 = jnp.bfloat16
MESH = pl.DeviceIdType.MESH

B = 64
S = 16
SLOT = 3
BAND = 8
ROWS = 256
PIECE = 2048
UNK = 16384
KS = 128
TOTAL = 262144
ZERO_BLOCK = 512


def split(x):
    hi = x.astype(bf16)
    return hi, (x - hi.astype(f32)).astype(bf16)


def stacked(x):
    hi, lo = split(x)
    return jnp.concatenate([hi, lo], 0)


def fold(x):
    return x[:S] + x[S:]


def wide(x):
    two = stacked(x)
    return jnp.concatenate([two, two], 1)


def dot(a, b):
    return jnp.dot(a, b, preferred_element_type=f32)


def dot_nt(a, b):
    return lax.dot_general(a, b, (((1,), (1,)), ((), ())), preferred_element_type=f32)


def kernel(
    columns, counts, blocks, vectors, basis,
    out, coeffs_out, factor_out,
    stage, weights, grid, expand, basis_stage, basis2, pieces, partial, arrived, product, twice, final,
    red_src, red_sib, red_row, red_col,
    load_sem, basis_sem, own_sem, out_sem,
    s1, r1, f1, s2, r2, s3, r3, sib_s, sib_r, row_s, row_r, col_s, col_r,
):
    row = lax.axis_index("row")
    col = lax.axis_index("col")
    yh, x, core = row // 8, row // 2 % 4, row % 2
    yl, z = col // 4, col % 4
    chip = yh * 4 + x
    sibling = (row + 1 - 2 * core, col)

    def row_peer(m):
        c = (yh + m // 4) % 2 * 4 + (x + m % 4) % 4
        return c, (c * 2 + core, col)

    def col_peer(m):
        k = (yl + m // 4) % 2 * 4 + (z + m % 4) % 4
        return k, (row, k)

    own_load = pltpu.make_async_copy(
        vectors.at[:, pl.ds(pl.multiple_of(col * PIECE, PIECE), PIECE)], pieces.at[row], own_sem
    )
    own_load.start()
    loads = []
    for s in range(SLOT):
        load = pltpu.make_async_copy(blocks.at[s], stage.at[s], load_sem.at[s])
        load.start()
        loads.append(load)

    def basis_load(c):
        return pltpu.make_async_copy(
            basis.at[:, pl.ds(c * PIECE, PIECE)], basis_stage.at[c % 2], basis_sem.at[c % 2]
        )

    basis_load(0).start()
    basis_load(1).start()

    barrier = pltpu.get_barrier_semaphore()
    peers = [sibling] + [row_peer(m)[1] for m in range(1, 8)] + [col_peer(m)[1] for m in range(1, 8)]
    for peer in peers:
        pl.semaphore_signal(barrier, inc=1, device_id=peer, device_id_type=MESH)
    pl.semaphore_wait(barrier, len(peers))

    own_load.wait()
    sends = []

    def send(src, dst, ssem, rsem, peer):
        copy = pltpu.make_async_remote_copy(src, dst, ssem, rsem, device_id=peer, device_id_type=MESH)
        copy.start()
        sends.append(copy)

    def arrival(dst, ssem, rsem):
        return pltpu.make_async_remote_copy(dst, dst, ssem, rsem, device_id=sibling, device_id_type=MESH)

    for m in (2, 6, 1, 3, 5, 7, 4):
        send(pieces.at[row], pieces.at[row], s1.at[m], r1.at[row], row_peer(m)[1])
    send(pieces.at[row], pieces.at[row], f1.at[0], r1.at[row], sibling)

    cell = lax.broadcasted_iota(jnp.int32, (128, 512), 0)
    spot = lax.broadcasted_iota(jnp.int32, (128, 512), 1)
    expand[...] = jnp.where(
        cell == spot // 256 * 64 + spot % 32 * 2 + spot // 128 % 2, 1.0, 0.0
    ).astype(bf16)
    grid[ZERO_BLOCK] = jnp.zeros((64, 128), bf16)

    for s in range(SLOT):
        loads[s].wait()

        @pl.loop(0, ROWS // BAND)
        def _(band, s=s):
            for i in range(BAND):
                hi, lo = split(stage[s, band, pl.ds(i, 32, stride=BAND), :])
                weights[band * BAND + i, 32 * s:32 * s + 32, :] = hi
                weights[band * BAND + i, 96 + 32 * s:128 + 32 * s, :] = lo

    own_basis = pl.multiple_of(col * 16, 16)
    gram_rows = jnp.zeros((2 * S, 2 * KS), f32)
    for c in range(8):
        basis_load(c).wait()
        chunk = stacked(basis_stage[c % 2])
        basis2[:, c * PIECE:(c + 1) * PIECE] = chunk
        if c + 2 < 8:
            basis_load(c + 2).start()
        left = jnp.concatenate(
            [
                basis2[pl.ds(own_basis, 16), c * PIECE:(c + 1) * PIECE],
                basis2[pl.ds(KS + own_basis, 16), c * PIECE:(c + 1) * PIECE],
            ],
            0,
        )
        gram_rows += dot_nt(left, chunk)

    def stage_sib(n, value):
        red_src[n, 0] = value
        send(red_src.at[n, 0], red_sib.at[n], sib_s.at[n], sib_r.at[n], sibling)

    def stage_row(n):
        arrival(red_sib.at[n], sib_s.at[n], sib_r.at[n]).wait_recv()
        red_row[n, chip] = red_src[n, 0] + red_sib[n]
        for m in range(1, 8):
            send(red_row.at[n, chip], red_row.at[n, chip], row_s.at[n, m], row_r.at[n, chip], row_peer(m)[1])

    def stage_col(n):
        for m in range(1, 8):
            c = row_peer(m)[0]
            arrival(red_row.at[n, c], row_s.at[n, m], row_r.at[n, c]).wait_recv()
        total = red_row[n, 0]
        for c in range(1, 8):
            total += red_row[n, c]
        red_col[n, col] = total * (1.0 / TOTAL)
        for m in range(1, 8):
            send(red_col.at[n, col], red_col.at[n, col], col_s.at[n, m], col_r.at[n, col], col_peer(m)[1])

    def stage_end(n):
        for m in range(1, 8):
            k = col_peer(m)[0]
            arrival(red_col.at[n, k], col_s.at[n, m], col_r.at[n, k]).wait_recv()

    def summed(n):
        total = red_col[n, 0]
        for k in range(1, 8):
            total += red_col[n, k]
        return total

    both = gram_rows[:, :KS] + gram_rows[:, KS:]
    stage_sib(0, fold(both))
    stage_row(0)

    def prepare(r):
        two = stacked(pieces[r])
        for h in range(4):
            left = jnp.concatenate([two[:, 128 * u:128 * u + 128] for u in range(4 * h, 4 * h + 4)], 0)
            spread = dot(left, expand[...]).astype(bf16)
            for u in range(4):
                for q in range(2):
                    for p in range(2):
                        lanes = (2 * q + p) * 128
                        grid[r * 32 + 2 * (4 * h + u) + q, 32 * p:32 * p + 32, :] = (
                            spread[32 * u:32 * u + 32, lanes:lanes + 128]
                        )

    prepare(row)
    order = (1, 3, 4, 2, 5, 7, 6)
    for n, m in enumerate(order):
        r = row_peer(m)[0] * 2 + core
        arrival(pieces.at[r], s1.at[m], r1.at[r]).wait_recv()
        send(pieces.at[r], pieces.at[r], f1.at[m], r1.at[r], sibling)
        prepare(r)
        q = row_peer(((0,) + order)[n])[0] * 2 + 1 - core
        arrival(pieces.at[q], f1.at[m], r1.at[q]).wait_recv()
        prepare(q)
    q = row_peer(order[-1])[0] * 2 + 1 - core
    arrival(pieces.at[q], f1.at[0], r1.at[q]).wait_recv()
    prepare(q)

    stage_col(0)

    low = lax.broadcasted_iota(jnp.int32, (S, 128), 1) < 64
    group = lax.broadcasted_iota(jnp.int32, (64, 128), 1) // 32

    def block_row(i):
        live = counts[0, i]
        where = []
        for t in range(SLOT):
            g = columns[t, i]
            where.append(jnp.where(live > t, g // ROWS * 32 + g % 32, ZERO_BLOCK))
        v0, v1, v2 = [grid[w] for w in where]
        first = jnp.where(group == 1, v1, jnp.where(group == 2, v2, v0))
        second = jnp.where(group == 0, v1, v2)
        left = jnp.concatenate([first, second], 1)[:, :192]
        res = dot(left, weights[i])
        return res[0:16] + res[16:32], res[32:48] + res[48:64]

    def piece(n, proj):
        m = 7 - n
        d = (yl + m // 4) % 2 * 4 + (z + m % 4) % 4
        for u in range(16):
            even0, odd0 = block_row(d * 32 + 2 * u)
            even1, odd1 = block_row(d * 32 + 2 * u + 1)
            partial[d, :, 128 * u:128 * u + 128] = jnp.where(low, even0, odd1) + pltpu.roll(
                jnp.where(low, even1, odd0), 64, 1
            )

        @pl.when(m > 0)
        def _():
            pltpu.make_async_remote_copy(
                partial.at[d], arrived.at[col], s2.at[m], r2.at[col], device_id=(row, d), device_id_type=MESH
            ).start()

        chunk = basis2[:, pl.ds(pl.multiple_of(d * PIECE, PIECE), PIECE)]
        return proj + dot_nt(stacked(partial[d]), chunk)

    proj = lax.fori_loop(0, 8, piece, jnp.zeros((2 * S, 2 * KS), f32))
    both = proj[:, :KS] + proj[:, KS:]
    stage_sib(1, fold(both))
    stage_row(1)
    stage_end(0)
    stage_col(1)

    total = partial[col]
    for m in range(1, 8):
        k = col_peer(m)[0]
        arrival(arrived.at[k], s2.at[m], r2.at[k]).wait_recv()
    for m in range(1, 8):
        total += arrived[col_peer(m)[0]]
    product[col] = total
    for m in (6, 2, 5, 7, 1, 3, 4):
        send(product.at[col], product.at[col], s3.at[m], r3.at[col], col_peer(m)[1])

    stage_end(1)
    first_proj = summed(1)
    basis_gram = jnp.concatenate([red_col[0, k] for k in range(8)], 0)
    coeffs = 2.0 * first_proj - jnp.dot(
        first_proj, basis_gram, precision=lax.Precision.HIGHEST, preferred_element_type=f32
    )
    coeffs_out[...] = coeffs
    coeffs2 = wide(coeffs)

    def remove(k):
        chunk = basis2[:, pl.ds(pl.multiple_of(k * PIECE, PIECE), PIECE)]
        rest = stacked(product[k] - fold(dot(coeffs2, chunk)))
        twice[k] = rest
        return rest

    own_rest = remove(col)
    quads = dot_nt(own_rest, own_rest)
    quads = quads[:, :S] + quads[:, S:]
    stage_sib(2, jnp.concatenate([fold(quads), jnp.zeros((S, 128 - S), f32)], 1))
    stage_row(2)
    stage_col(2)
    for m in (1, 3, 4, 2, 5, 7, 6):
        k = col_peer(m)[0]
        arrival(product.at[k], s3.at[m], r3.at[k]).wait_recv()
        remove(k)
    stage_end(2)

    lane = lax.broadcasted_iota(jnp.int32, (S, 128), 1)
    line = lax.broadcasted_iota(jnp.int32, (S, 128), 0)
    work = jnp.where(lane == line + S, 1.0, summed(2))
    factor = jnp.zeros((S, 128), f32)
    scale = jnp.zeros((S, 128), f32)
    for j in range(S):
        column = jnp.broadcast_to(work[:, j:j + 1], (S, 128))
        pivot = jnp.broadcast_to(column[j:j + 1, :], (S, 128))
        root = lax.rsqrt(pivot)
        factor = jnp.where((lane == j) & (line >= j), column * root, factor)
        scale = jnp.where(line == j, root, scale)
        ratio = jnp.where(line > j, column / pivot, 0.0)
        work = work - ratio * jnp.broadcast_to(work[j:j + 1, :], (S, 128))
    factor_out[...] = factor[:, :S]
    inverse = (work * scale)[:, S:2 * S]
    inverse2 = wide(inverse)
    writes = []
    for k in range(8):
        final[k] = fold(dot(inverse2, twice[k]))
        write = pltpu.make_async_copy(final.at[k], out.at[:, pl.ds(k * PIECE, PIECE)], out_sem.at[k])
        write.start()
        writes.append(write)

    for copy in sends:
        copy.wait_send()
    for m in range(1, 8):
        arrival(partial.at[col_peer(m)[0]], s2.at[m], r2.at[col]).wait_send()
    for write in writes:
        write.wait()


def body(blocks, columns, counts, old_basis, vectors):
    bands = blocks.reshape(ROWS // BAND, BAND, SLOT, 32, 128).transpose(2, 0, 3, 1, 4)
    bands = bands.reshape(SLOT, ROWS // BAND, 32 * BAND, 128)
    D = pltpu.SemaphoreType.DMA
    V = pltpu.VMEM
    any_space = pl.BlockSpec(memory_space=pl.ANY)
    smem = pl.BlockSpec(memory_space=pltpu.SMEM)
    vmem = pl.BlockSpec(memory_space=pltpu.VMEM)
    new_block, coeffs, factor = pl.pallas_call(
        kernel,
        out_shape=(
            jax.ShapeDtypeStruct((S, UNK), f32),
            jax.ShapeDtypeStruct((S, KS), f32),
            jax.ShapeDtypeStruct((S, S), f32),
        ),
        in_specs=[smem, smem, any_space, any_space, any_space],
        out_specs=(any_space, vmem, vmem),
        scratch_shapes=[
            V((SLOT, ROWS // BAND, 32 * BAND, 128), f32),
            V((ROWS, 192, 128), bf16),
            V((ZERO_BLOCK + 1, 64, 128), bf16),
            V((128, 512), bf16),
            V((2, KS, PIECE), f32),
            V((2 * KS, UNK), bf16),
            V((16, S, PIECE), f32),
            V((8, S, PIECE), f32),
            V((8, S, PIECE), f32),
            V((8, S, PIECE), f32),
            V((8, 2 * S, PIECE), bf16),
            V((8, S, PIECE), f32),
            V((3, 1, S, 128), f32),
            V((3, S, 128), f32),
            V((3, 8, S, 128), f32),
            V((3, 8, S, 128), f32),
            D((SLOT,)), D((2,)), D, D((8,)),
            D((8,)), D((16,)), D((8,)), D((8,)), D((8,)), D((8,)), D((8,)),
            D((3,)), D((3,)), D((3, 8)), D((3, 8)), D((3, 8)), D((3, 8)),
        ],
        compiler_params=pltpu.CompilerParams(
            collective_id=0, has_side_effects=True, vmem_limit_bytes=62 << 20
        ),
    )(columns.T, counts.T, bands, vectors, old_basis)
    return new_block, coeffs.T, factor


def solution(mesh):
    return jax.shard_map(
        body,
        mesh=mesh,
        in_specs=(
            P("row", "col", None),
            P("row", "col"),
            P("row", "col"),
            P(None, "row"),
            P(None, "row"),
        ),
        out_specs=(P(None, "row"), P(), P()),
        check_vma=False,
    )
```

time: 333 us -> 76.6 us (0.23)
  blocking collectives: 106 us -> 0 us
  waiting for transfers between devices: 88 us -> 0 us
  Pallas kernels: 0 us -> 69.9 us
  matrix products: 61 us -> 0 us
  local copies, waits for them, and re-layouts: 57.7 us -> 4.85 us
  between operations: 14.2 us -> 0.64 us
  other arithmetic: 5.35 us -> 0 us
    psum x3 -> x0, blocking collectives: 106 us -> none  [reduce_small(): return lax.psum(terms, 'row')]
    psum x1 -> x0, waiting for transfers between devices: 70.8 us -> none  [body(): product = lax.psum(partial_rows, 'col')]
    pallas_call x0 -> x1, Pallas kernels: none -> 69.9 us  [body(): pl.pallas_call(kernel, out_shape=(jax.ShapeDtypeStruct((S, UNK), f32), ja...]
    dot_general x6 -> x0, matrix products: 58.9 us -> none  [the longest x1 26.4 us: body(): jnp.einsum('nrsb,rsba->nra', taken * live_mask[None, :, :, None], block_m...]
    reshape x4 -> x0, local copies, waits for them, and re-layouts: 35.9 us -> none  [the longest x1 23.5 us: body(): block_mats = blocks.reshape(rows_dev, SLOT, B, B)]
    all_gather x1 -> x0, waiting for transfers between devices: 17.2 us -> none  [body(): pieces = lax.all_gather(mine, 'row', axis=1, tiled=True)]
    unnamed x11 -> x3, local copies, waits for them, and re-layouts: 13.8 us -> 4.85 us
    gather x1 -> x0, local copies, waits for them, and re-layouts: 6.09 us -> none  [body(): taken = jnp.take(vector_grid, local_ids, axis=1)]
  transfers between devices with their start and end apart: 2 -> 0, of which waited for: 2 -> 0; matrix products, arithmetic and copies ran while one was open for 11% -> 0% of each run, Pallas kernels for 0% -> 0%
where the time goes in v1:
time: 76.6 us; the launch traced here: 75.4 us
  Pallas kernels  69.9 us (91%)
  local copies, waits for them, and re-layouts  4.85 us (6%)
    pallas_call x1, Pallas kernels, body(): pl.pallas_call(kernel, out_shape=(jax.ShapeDtypeStruct((S, UNK), f32), ja...  69.9 us
    unnamed x3, local copies, waits for them, and re-layouts  4.85 us

profile of v1, /device:TPU:1, one launch (start us, length us, event | category | flops | bytes accessed | tf_op | source)
XLA Modules:
  0.0 75.4 jit_solution(14055413854587958751)
XLA Ops:
  0.6 69.9 %shard_map.76 = (f32[16,16384]{1,0:T(8,128)}, f32[16,128]{1,0:T(8,128)}, f32[16,16]{1,0:T(8,128)}) custom-call(s32[3,256]{1,0:T(4,128)} %bitcast.10, s32[1,256]{1,0:T(1,128)} %bitcast.11, f32[3,32,256,128]{3,2,1,0:T(8,128)} %bitcast.8, f32[16,16384]{1,0:T(8,128)} %vectors.1, f32[128,16384]{1,0:T(8,128)} %basis.1), custom_call_target="tpu_custom_call" | custom-call | tf_op jit(solution)/shard_map/pallas_call | solution.py:332
  70.6 2.3 %copy.11 = f32[16,16384]{1,0:T(8,128)} copy(f32[16,16384]{1,0:T(8,128)} %get-tuple-element.12) | data formatting | bytes 2097152
  72.8 1.3 %copy.12 = f32[128,16]{0,1:T(8,128)} copy(f32[128,16]{0,1:T(8,128)} %bitcast.9) | data formatting | bytes 16384
  74.1 1.3 %copy.13 = f32[16,16]{1,0:T(8,128)} copy(f32[16,16]{1,0:T(8,128)} %get-tuple-element.14) | data formatting | bytes 2048

commit v2 on v1

--- a/solution.py
+++ b/solution.py
@@ -52,11 +52,11 @@
 
 def kernel(
     columns, counts, blocks, vectors, basis,
-    out, coeffs_out, factor_out,
-    stage, weights, grid, expand, basis_stage, basis2, pieces, partial, arrived, product, twice, final,
+    twice_out, coeffs_out, factor_out, inverse_out,
+    stage, weights, grid, expand, basis_stage, basis2, pieces, partial, arrived, product, twice,
     red_src, red_sib, red_row, red_col,
     load_sem, basis_sem, own_sem, out_sem,
-    s1, r1, f1, s2, r2, s3, r3, sib_s, sib_r, row_s, row_r, col_s, col_r,
+    s1, r1, s2, r2, s3, r3, sib_s, sib_r, row_s, row_r, col_s, col_r,
 ):
     row = lax.axis_index("row")
     col = lax.axis_index("col")
@@ -73,10 +73,16 @@
         k = (yl + m // 4) % 2 * 4 + (z + m % 4) % 4
         return k, (row, k)
 
-    own_load = pltpu.make_async_copy(
-        vectors.at[:, pl.ds(pl.multiple_of(col * PIECE, PIECE), PIECE)], pieces.at[row], own_sem
-    )
-    own_load.start()
+    own_loads = []
+    for h in range(2):
+        own_loads.append(
+            pltpu.make_async_copy(
+                vectors.at[8 * h:8 * h + 8, pl.ds(pl.multiple_of(col * PIECE, PIECE), PIECE)],
+                pieces.at[h, row],
+                own_sem.at[h],
+            )
+        )
+        own_loads[h].start()
     loads = []
     for s in range(SLOT):
         load = pltpu.make_async_copy(blocks.at[s], stage.at[s], load_sem.at[s])
@@ -95,22 +101,6 @@
     peers = [sibling] + [row_peer(m)[1] for m in range(1, 8)] + [col_peer(m)[1] for m in range(1, 8)]
     for peer in peers:
         pl.semaphore_signal(barrier, inc=1, device_id=peer, device_id_type=MESH)
-    pl.semaphore_wait(barrier, len(peers))
-
-    own_load.wait()
-    sends = []
-
-    def send(src, dst, ssem, rsem, peer):
-        copy = pltpu.make_async_remote_copy(src, dst, ssem, rsem, device_id=peer, device_id_type=MESH)
-        copy.start()
-        sends.append(copy)
-
-    def arrival(dst, ssem, rsem):
-        return pltpu.make_async_remote_copy(dst, dst, ssem, rsem, device_id=sibling, device_id_type=MESH)
-
-    for m in (2, 6, 1, 3, 5, 7, 4):
-        send(pieces.at[row], pieces.at[row], s1.at[m], r1.at[row], row_peer(m)[1])
-    send(pieces.at[row], pieces.at[row], f1.at[0], r1.at[row], sibling)
 
     cell = lax.broadcasted_iota(jnp.int32, (128, 512), 0)
     spot = lax.broadcasted_iota(jnp.int32, (128, 512), 1)
@@ -128,6 +118,44 @@
                 hi, lo = split(stage[s, band, pl.ds(i, 32, stride=BAND), :])
                 weights[band * BAND + i, 32 * s:32 * s + 32, :] = hi
                 weights[band * BAND + i, 96 + 32 * s:128 + 32 * s, :] = lo
+
+    pl.semaphore_wait(barrier, len(peers))
+
+    sends = []
+
+    def send(src, dst, ssem, rsem, peer):
+        copy = pltpu.make_async_remote_copy(src, dst, ssem, rsem, device_id=peer, device_id_type=MESH)
+        copy.start()
+        sends.append(copy)
+
+    def arrival(dst, ssem, rsem):
+        return pltpu.make_async_remote_copy(dst, dst, ssem, rsem, device_id=sibling, device_id_type=MESH)
+
+    def pass_on(h, r, n, peer):
+        send(pieces.at[h, r], pieces.at[h, r], s1.at[h, n], r1.at[h, r], peer)
+
+    for h in range(2):
+        own_loads[h].wait()
+        for m in (4, 2):
+            pass_on(h, row, m, row_peer(m)[1])
+    for h in range(2):
+        for m in (1, 3):
+            pass_on(h, row, m, row_peer(m)[1])
+        pass_on(h, row, 0, sibling)
+
+    def take(h, m):
+        r = row_peer(m)[0] * 2 + core
+        arrival(pieces.at[h, r], s1.at[h, 0], r1.at[h, r]).wait_recv()
+        if m == 4:
+            pass_on(h, r, 8, row_peer(1)[1])
+            pass_on(h, r, 9, row_peer(3)[1])
+        if m == 2:
+            pass_on(h, r, 10, row_peer(4)[1])
+        pass_on(h, r, 10 + m, sibling)
+
+    def take_sibling(h, m):
+        r = row_peer(m)[0] * 2 + 1 - core
+        arrival(pieces.at[h, r], s1.at[h, 0], r1.at[h, r]).wait_recv()
 
     own_basis = pl.multiple_of(col * 16, 16)
     gram_rows = jnp.zeros((2 * S, 2 * KS), f32)
@@ -183,7 +211,7 @@
     stage_row(0)
 
     def prepare(r):
-        two = stacked(pieces[r])
+        two = stacked(jnp.concatenate([pieces[0, r], pieces[1, r]], 0))
         for h in range(4):
             left = jnp.concatenate([two[:, 128 * u:128 * u + 128] for u in range(4 * h, 4 * h + 4)], 0)
             spread = dot(left, expand[...]).astype(bf16)
@@ -195,19 +223,28 @@
                             spread[32 * u:32 * u + 32, lanes:lanes + 128]
                         )
 
+    for h in range(2):
+        for m in (4, 2, 1, 3):
+            take(h, m)
+    for h in range(2):
+        take_sibling(h, 0)
     prepare(row)
-    order = (1, 3, 4, 2, 5, 7, 6)
-    for n, m in enumerate(order):
-        r = row_peer(m)[0] * 2 + core
-        arrival(pieces.at[r], s1.at[m], r1.at[r]).wait_recv()
-        send(pieces.at[r], pieces.at[r], f1.at[m], r1.at[r], sibling)
-        prepare(r)
-        q = row_peer(((0,) + order)[n])[0] * 2 + 1 - core
-        arrival(pieces.at[q], f1.at[m], r1.at[q]).wait_recv()
-        prepare(q)
-    q = row_peer(order[-1])[0] * 2 + 1 - core
-    arrival(pieces.at[q], f1.at[0], r1.at[q]).wait_recv()
-    prepare(q)
+    prepare(row + 1 - 2 * core)
+    for m in (4, 2, 1, 3):
+        prepare(row_peer(m)[0] * 2 + core)
+    for m in (5, 7, 6):
+        take(0, m)
+    for m in (4, 2, 1, 3):
+        for h in range(2):
+            take_sibling(h, m)
+        prepare(row_peer(m)[0] * 2 + 1 - core)
+    for m in (5, 7, 6):
+        take(1, m)
+        prepare(row_peer(m)[0] * 2 + core)
+    for m in (5, 7, 6):
+        for h in range(2):
+            take_sibling(h, m)
+        prepare(row_peer(m)[0] * 2 + 1 - core)
 
     stage_col(0)
 
@@ -219,7 +256,8 @@
         where = []
         for t in range(SLOT):
             g = columns[t, i]
-            where.append(jnp.where(live > t, g // ROWS * 32 + g % 32, ZERO_BLOCK))
+            high = lax.shift_left(lax.shift_right_logical(g, 8), 5)
+            where.append(jnp.where(live > t, high + jnp.bitwise_and(g, 31), ZERO_BLOCK))
         v0, v1, v2 = [grid[w] for w in where]
         first = jnp.where(group == 1, v1, jnp.where(group == 2, v2, v0))
         second = jnp.where(group == 0, v1, v2)
@@ -228,7 +266,9 @@
         return res[0:16] + res[16:32], res[32:48] + res[48:64]
 
     def piece(n, proj):
-        m = 7 - n
+        m = n * 0
+        for place, peer in enumerate((6, 5, 2, 7, 1, 4, 3)):
+            m = jnp.where(n == place, peer, m)
         d = (yl + m // 4) % 2 * 4 + (z + m % 4) % 4
         for u in range(16):
             even0, odd0 = block_row(d * 32 + 2 * u)
@@ -271,23 +311,40 @@
     )
     coeffs_out[...] = coeffs
     coeffs2 = wide(coeffs)
-
-    def remove(k):
+    writes = []
+
+    def seen(k):
         chunk = basis2[:, pl.ds(pl.multiple_of(k * PIECE, PIECE), PIECE)]
-        rest = stacked(product[k] - fold(dot(coeffs2, chunk)))
+        return fold(dot(coeffs2, chunk))
+
+    def keep(k, rest):
+        rest = stacked(rest)
         twice[k] = rest
+        write = pltpu.make_async_copy(twice.at[k], twice_out.at[k], out_sem.at[k])
+        write.start()
+        writes.append(write)
         return rest
 
-    own_rest = remove(col)
+    def remove(m):
+        k = col_peer(m)[0]
+        arrival(product.at[k], s3.at[m], r3.at[k]).wait_recv()
+        keep(k, product[k] - arrived[k])
+
+    def foresee(*ms):
+        for m in ms:
+            arrived[col_peer(m)[0]] = seen(col_peer(m)[0])
+
+    own_rest = keep(col, product[col] - seen(col))
     quads = dot_nt(own_rest, own_rest)
     quads = quads[:, :S] + quads[:, S:]
     stage_sib(2, jnp.concatenate([fold(quads), jnp.zeros((S, 128 - S), f32)], 1))
+    foresee(1, 3)
     stage_row(2)
+    foresee(4, 5, 7)
     stage_col(2)
-    for m in (1, 3, 4, 2, 5, 7, 6):
-        k = col_peer(m)[0]
-        arrival(product.at[k], s3.at[m], r3.at[k]).wait_recv()
-        remove(k)
+    foresee(2, 6)
+    for m in (1, 3, 4):
+        remove(m)
     stage_end(2)
 
     lane = lax.broadcasted_iota(jnp.int32, (S, 128), 1)
@@ -304,19 +361,34 @@
         ratio = jnp.where(line > j, column / pivot, 0.0)
         work = work - ratio * jnp.broadcast_to(work[j:j + 1, :], (S, 128))
     factor_out[...] = factor[:, :S]
-    inverse = (work * scale)[:, S:2 * S]
-    inverse2 = wide(inverse)
-    writes = []
+    inverse_out[...] = work * scale
+
+    for m in (5, 7, 2, 6):
+        remove(m)
+
+    for copy in sends:
+        copy.wait_send()
+    for m in range(1, 8):
+        arrival(partial.at[col_peer(m)[0]], s2.at[m], r2.at[col]).wait_send()
+    for write in writes:
+        write.wait()
+
+
+def finish(twice_in, coeffs_in, factor_in, inverse_in, out, coeffs_out, factor_out, twice, final, in_sem, out_sem, small_sem):
+    loads, writes = [], []
     for k in range(8):
+        loads.append(pltpu.make_async_copy(twice_in.at[k], twice.at[k], in_sem.at[k]))
+    writes.append(pltpu.make_async_copy(coeffs_in, coeffs_out, small_sem.at[0]))
+    writes.append(pltpu.make_async_copy(factor_in, factor_out, small_sem.at[1]))
+    for copy in loads + writes:
+        copy.start()
+    inverse2 = wide(inverse_in[...][:, S:2 * S])
+    for k in range(8):
+        loads[k].wait()
         final[k] = fold(dot(inverse2, twice[k]))
         write = pltpu.make_async_copy(final.at[k], out.at[:, pl.ds(k * PIECE, PIECE)], out_sem.at[k])
         write.start()
         writes.append(write)
-
-    for copy in sends:
-        copy.wait_send()
-    for m in range(1, 8):
-        arrival(partial.at[col_peer(m)[0]], s2.at[m], r2.at[col]).wait_send()
     for write in writes:
         write.wait()
 
@@ -329,15 +401,16 @@
     any_space = pl.BlockSpec(memory_space=pl.ANY)
     smem = pl.BlockSpec(memory_space=pltpu.SMEM)
     vmem = pl.BlockSpec(memory_space=pltpu.VMEM)
-    new_block, coeffs, factor = pl.pallas_call(
+    twice, coeffs, factor, inverse = pl.pallas_call(
         kernel,
         out_shape=(
-            jax.ShapeDtypeStruct((S, UNK), f32),
+            jax.ShapeDtypeStruct((8, 2 * S, PIECE), bf16),
             jax.ShapeDtypeStruct((S, KS), f32),
             jax.ShapeDtypeStruct((S, S), f32),
+            jax.ShapeDtypeStruct((S, 128), f32),
         ),
         in_specs=[smem, smem, any_space, any_space, any_space],
-        out_specs=(any_space, vmem, vmem),
+        out_specs=(any_space, vmem, vmem, vmem),
         scratch_shapes=[
             V((SLOT, ROWS // BAND, 32 * BAND, 128), f32),
             V((ROWS, 192, 128), bf16),
@@ -345,24 +418,35 @@
             V((128, 512), bf16),
             V((2, KS, PIECE), f32),
             V((2 * KS, UNK), bf16),
-            V((16, S, PIECE), f32),
+            V((2, 16, S // 2, PIECE), f32),
             V((8, S, PIECE), f32),
             V((8, S, PIECE), f32),
             V((8, S, PIECE), f32),
             V((8, 2 * S, PIECE), bf16),
-            V((8, S, PIECE), f32),
             V((3, 1, S, 128), f32),
             V((3, S, 128), f32),
             V((3, 8, S, 128), f32),
             V((3, 8, S, 128), f32),
-            D((SLOT,)), D((2,)), D, D((8,)),
-            D((8,)), D((16,)), D((8,)), D((8,)), D((8,)), D((8,)), D((8,)),
+            D((SLOT,)), D((2,)), D((2,)), D((8,)),
+            D((2, 18)), D((2, 16)), D((8,)), D((8,)), D((8,)), D((8,)),
             D((3,)), D((3,)), D((3, 8)), D((3, 8)), D((3, 8)), D((3, 8)),
         ],
         compiler_params=pltpu.CompilerParams(
             collective_id=0, has_side_effects=True, vmem_limit_bytes=62 << 20
         ),
     )(columns.T, counts.T, bands, vectors, old_basis)
+    new_block, coeffs, factor = pl.pallas_call(
+        finish,
+        out_shape=(
+            jax.ShapeDtypeStruct((S, UNK), f32),
+            jax.ShapeDtypeStruct((S, KS), f32),
+            jax.ShapeDtypeStruct((S, S), f32),
+        ),
+        in_specs=[any_space, any_space, any_space, vmem],
+        out_specs=(any_space, any_space, any_space),
+        scratch_shapes=[V((8, 2 * S, PIECE), bf16), V((8, S, PIECE), f32), D((8,)), D((8,)), D((2,))],
+        compiler_params=pltpu.CompilerParams(vmem_limit_bytes=62 << 20),
+    )(twice, coeffs, factor, inverse)
     return new_block, coeffs.T, factor
 
 

time: 76.6 us -> 73.9 us (0.965); the launches traced: 75.4 us -> 73.6 us
  local copies, waits for them, and re-layouts: 4.85 us -> 0 us
  Pallas kernels: 69.9 us -> 72.8 us
    unnamed x3 -> x0, local copies, waits for them, and re-layouts: 4.85 us -> none
    pallas_call x1 -> x2, Pallas kernels: 69.9 us -> 72.8 us  [the longest x1 69 us: body(): pl.pallas_call(kernel, out_shape=(jax.ShapeDtypeStruct((8, 2 * S, PIECE),...]
where the time goes in v2:
time: 73.9 us; the launch traced here: 73.6 us
  Pallas kernels  72.8 us (99%)
  between operations  0.8 us (1%)
    pallas_call x1, Pallas kernels, body(): pl.pallas_call(kernel, out_shape=(jax.ShapeDtypeStruct((8, 2 * S, PIECE),...  69 us
    pallas_call x1, Pallas kernels, body(): pl.pallas_call(finish, out_shape=(jax.ShapeDtypeStruct((S, UNK), f32), ja...  3.76 us

profile of v2, /device:TPU:1, one launch (start us, length us, event | category | flops | bytes accessed | tf_op | source)
XLA Modules:
  0.0 73.6 jit_solution(11642223358527198841)
XLA Ops:
  0.6 69.0 %shard_map.76 = (bf16[8,32,2048]{2,1,0:T(8,128)(2,1)}, f32[16,128]{1,0:T(8,128)}, f32[16,16]{1,0:T(8,128)}, f32[16,128]{1,0:T(8,128)}) custom-call(s32[3,256]{1,0:T(4,128)} %bitcast.9, s32[1,256]{1,0:T(1,128)} %bitcast.10, f32[3,32,256,128]{3,2,1,0:T(8,128)} %bitcast.8, f32[16,16384]{1,0:T(8,128)} %vectors.1, f32[128,16384]{1,0:T(8,128)} %basis.1), custom_call_target="tpu_custom_call" | custom-call | tf_op jit(solution)/shard_map/pallas_call | solution.py:404
  69.7 3.8 %shard_map.77 = (f32[16,16384]{1,0:T(8,128)}, f32[16,128]{1,0:T(8,128)}, f32[16,16]{1,0:T(8,128)}) custom-call(bf16[8,32,2048]{2,1,0:T(8,128)(2,1)} %get-tuple-element.10.twice_in, f32[16,128]{1,0:T(8,128)} %get-tuple-element.11.coeffs_in, f32[16,16]{1,0:T(8,128)} %get-tuple-element.12.factor_in, f32[16,128]{1,0:T(8,128)} %get-tuple-element.13.inverse_in), custom_call_target="tpu_custom_call" | custom-call | tf_op jit(solution)/shard_map/pallas_call | solution.py:438

commit v3 on v2

--- a/solution.py
+++ b/solution.py
@@ -53,7 +53,7 @@
 def kernel(
     columns, counts, blocks, vectors, basis,
     twice_out, coeffs_out, factor_out, inverse_out,
-    stage, weights, grid, expand, basis_stage, basis2, pieces, partial, arrived, product, twice,
+    stage, weights, grid, expand, basis_stage, basis2, pieces, partial, inbox, relay, foreseen, product, twice,
     red_src, red_sib, red_row, red_col,
     load_sem, basis_sem, own_sem, out_sem,
     s1, r1, s2, r2, s3, r3, sib_s, sib_r, row_s, row_r, col_s, col_r,
@@ -265,9 +265,18 @@
         res = dot(left, weights[i])
         return res[0:16] + res[16:32], res[32:48] + res[48:64]
 
+    def sum_copy(src, m, dy, dz):
+        return pltpu.make_async_remote_copy(
+            src, inbox.at[m], s2.at[m], r2.at[m],
+            device_id=(row, (yl + dy) % 2 * 4 + (z + dz) % 4), device_id_type=MESH,
+        )
+
+    def landed(m):
+        sum_copy(inbox.at[m], m, 1, 0).wait_recv()
+
     def piece(n, proj):
         m = n * 0
-        for place, peer in enumerate((6, 5, 2, 7, 1, 4, 3)):
+        for place, peer in enumerate((6, 5, 7, 1, 3, 2, 4)):
             m = jnp.where(n == place, peer, m)
         d = (yl + m // 4) % 2 * 4 + (z + m % 4) % 4
         for u in range(16):
@@ -277,11 +286,26 @@
                 jnp.where(low, even1, odd0), 64, 1
             )
 
-        @pl.when(m > 0)
+        @pl.when(n == 0)
         def _():
-            pltpu.make_async_remote_copy(
-                partial.at[d], arrived.at[col], s2.at[m], r2.at[col], device_id=(row, d), device_id_type=MESH
-            ).start()
+            sum_copy(partial.at[d], 6, 1, 0).start()
+
+        @pl.when((n >= 1) & (n < 5))
+        def _():
+            sum_copy(partial.at[d], m, 0, m % 4).start()
+
+        @pl.when(n == 5)
+        def _():
+            landed(6)
+            relay[0] = partial[d] + inbox[6]
+            sum_copy(relay.at[0], 2, 0, 2).start()
+
+        @pl.when(n == 6)
+        def _():
+            landed(5)
+            landed(7)
+            relay[1] = partial[d] + (inbox[5] + inbox[7])
+            sum_copy(relay.at[1], 4, 1, 0).start()
 
         chunk = basis2[:, pl.ds(pl.multiple_of(d * PIECE, PIECE), PIECE)]
         return proj + dot_nt(stacked(partial[d]), chunk)
@@ -293,15 +317,22 @@
     stage_end(0)
     stage_col(1)
 
-    total = partial[col]
-    for m in range(1, 8):
-        k = col_peer(m)[0]
-        arrival(arrived.at[k], s2.at[m], r2.at[k]).wait_recv()
-    for m in range(1, 8):
-        total += arrived[col_peer(m)[0]]
+    for m in (1, 3, 2, 4):
+        landed(m)
+    total = partial[col] + (inbox[1] + inbox[3]) + (inbox[2] + inbox[4])
+
+    def spread(h, k, n, m):
+        rows = pl.ds(8 * h, 8)
+        send(product.at[k, rows], product.at[k, rows], s3.at[h, n], r3.at[h, k], col_peer(m)[1])
+
+    def spread_wait(h, k):
+        rows = pl.ds(8 * h, 8)
+        arrival(product.at[k, rows], s3.at[h, 0], r3.at[h, k]).wait_recv()
+
     product[col] = total
-    for m in (6, 2, 5, 7, 1, 3, 4):
-        send(product.at[col], product.at[col], s3.at[m], r3.at[col], col_peer(m)[1])
+    for m in (4, 2, 1, 3):
+        for h in range(2):
+            spread(h, col, m, m)
 
     stage_end(1)
     first_proj = summed(1)
@@ -327,23 +358,33 @@
 
     def remove(m):
         k = col_peer(m)[0]
-        arrival(product.at[k], s3.at[m], r3.at[k]).wait_recv()
-        keep(k, product[k] - arrived[k])
+        if m not in (2, 4):
+            for h in range(2):
+                spread_wait(h, k)
+        keep(k, product[k] - foreseen[k])
 
     def foresee(*ms):
         for m in ms:
-            arrived[col_peer(m)[0]] = seen(col_peer(m)[0])
+            foreseen[col_peer(m)[0]] = seen(col_peer(m)[0])
 
     own_rest = keep(col, product[col] - seen(col))
     quads = dot_nt(own_rest, own_rest)
     quads = quads[:, :S] + quads[:, S:]
     stage_sib(2, jnp.concatenate([fold(quads), jnp.zeros((S, 128 - S), f32)], 1))
-    foresee(1, 3)
+    for h in range(2):
+        k = col_peer(4)[0]
+        spread_wait(h, k)
+        spread(h, k, 5, 1)
+        spread(h, k, 6, 3)
     stage_row(2)
-    foresee(4, 5, 7)
+    for h in range(2):
+        k = col_peer(2)[0]
+        spread_wait(h, k)
+        spread(h, k, 7, 4)
+    foresee(1, 3, 4, 2)
     stage_col(2)
-    foresee(2, 6)
-    for m in (1, 3, 4):
+    foresee(5, 7, 6)
+    for m in (1, 3, 4, 2):
         remove(m)
     stage_end(2)
 
@@ -363,13 +404,13 @@
     factor_out[...] = factor[:, :S]
     inverse_out[...] = work * scale
 
-    for m in (5, 7, 2, 6):
+    for m in (5, 7, 6):
         remove(m)
 
     for copy in sends:
         copy.wait_send()
     for m in range(1, 8):
-        arrival(partial.at[col_peer(m)[0]], s2.at[m], r2.at[col]).wait_send()
+        sum_copy(inbox.at[m], m, 1, 0).wait_send()
     for write in writes:
         write.wait()
 
@@ -421,6 +462,8 @@
             V((2, 16, S // 2, PIECE), f32),
             V((8, S, PIECE), f32),
             V((8, S, PIECE), f32),
+            V((2, S, PIECE), f32),
+            V((8, S, PIECE), f32),
             V((8, S, PIECE), f32),
             V((8, 2 * S, PIECE), bf16),
             V((3, 1, S, 128), f32),
@@ -428,7 +471,7 @@
             V((3, 8, S, 128), f32),
             V((3, 8, S, 128), f32),
             D((SLOT,)), D((2,)), D((2,)), D((8,)),
-            D((2, 18)), D((2, 16)), D((8,)), D((8,)), D((8,)), D((8,)),
+            D((2, 18)), D((2, 16)), D((8,)), D((8,)), D((2, 8)), D((2, 8)),
             D((3,)), D((3,)), D((3, 8)), D((3, 8)), D((3, 8)), D((3, 8)),
         ],
         compiler_params=pltpu.CompilerParams(

time: 73.9 us -> 68.1 us (0.922)
  Pallas kernels: 72.8 us -> 67 us
    pallas_call x1, Pallas kernels: 69 us -> 63.3 us  [body(): pl.pallas_call(kernel, out_shape=(jax.ShapeDtypeStruct((8, 2 * S, PIECE),...]
where the time goes in v3:
time: 68.1 us; the launch traced here: 67.8 us
  Pallas kernels  67 us (98%)
  between operations  0.8 us (1%)
    pallas_call x1, Pallas kernels, body(): pl.pallas_call(kernel, out_shape=(jax.ShapeDtypeStruct((8, 2 * S, PIECE),...  63.3 us
    pallas_call x1, Pallas kernels, body(): pl.pallas_call(finish, out_shape=(jax.ShapeDtypeStruct((S, UNK), f32), ja...  3.76 us

profile of v3, /device:TPU:1, one launch (start us, length us, event | category | flops | bytes accessed | tf_op | source)
XLA Modules:
  0.0 67.8 jit_solution(9985346751776084838)
XLA Ops:
  0.6 63.3 %shard_map.76 = (bf16[8,32,2048]{2,1,0:T(8,128)(2,1)}, f32[16,128]{1,0:T(8,128)}, f32[16,16]{1,0:T(8,128)}, f32[16,128]{1,0:T(8,128)}) custom-call(s32[3,256]{1,0:T(4,128)} %bitcast.9, s32[1,256]{1,0:T(1,128)} %bitcast.10, f32[3,32,256,128]{3,2,1,0:T(8,128)} %bitcast.8, f32[16,16384]{1,0:T(8,128)} %vectors.1, f32[128,16384]{1,0:T(8,128)} %basis.1), custom_call_target="tpu_custom_call" | custom-call | tf_op jit(solution)/shard_map/pallas_call | solution.py:445
  63.9 3.8 %shard_map.77 = (f32[16,16384]{1,0:T(8,128)}, f32[16,128]{1,0:T(8,128)}, f32[16,16]{1,0:T(8,128)}) custom-call(bf16[8,32,2048]{2,1,0:T(8,128)(2,1)} %get-tuple-element.10.twice_in, f32[16,128]{1,0:T(8,128)} %get-tuple-element.11.coeffs_in, f32[16,16]{1,0:T(8,128)} %get-tuple-element.12.factor_in, f32[16,128]{1,0:T(8,128)} %get-tuple-element.13.inverse_in), custom_call_target="tpu_custom_call" | custom-call | tf_op jit(solution)/shard_map/pallas_call | solution.py:481

commit v4 on v3

--- a/solution.py
+++ b/solution.py
@@ -48,6 +48,16 @@
 
 def dot_nt(a, b):
     return lax.dot_general(a, b, (((1,), (1,)), ((), ())), preferred_element_type=f32)
+
+
+def exact(a, b):
+    return jnp.dot(a, b, precision=lax.Precision.HIGHEST, preferred_element_type=f32)
+
+
+def exact_nt(a, b):
+    return lax.dot_general(
+        a, b, (((1,), (1,)), ((), ())), precision=lax.Precision.HIGHEST, preferred_element_type=f32
+    )
 
 
 def kernel(
@@ -274,11 +284,15 @@
     def landed(m):
         sum_copy(inbox.at[m], m, 1, 0).wait_recv()
 
-    def piece(n, proj):
+    def turn(n):
         m = n * 0
         for place, peer in enumerate((6, 5, 7, 1, 3, 2, 4)):
             m = jnp.where(n == place, peer, m)
-        d = (yl + m // 4) % 2 * 4 + (z + m % 4) % 4
+        return m, (yl + m // 4) % 2 * 4 + (z + m % 4) % 4
+
+    @pl.loop(0, 8)
+    def _(n):
+        m, d = turn(n)
         for u in range(16):
             even0, odd0 = block_row(d * 32 + 2 * u)
             even1, odd1 = block_row(d * 32 + 2 * u + 1)
@@ -294,29 +308,23 @@
         def _():
             sum_copy(partial.at[d], m, 0, m % 4).start()
 
-        @pl.when(n == 5)
-        def _():
-            landed(6)
-            relay[0] = partial[d] + inbox[6]
-            sum_copy(relay.at[0], 2, 0, 2).start()
-
-        @pl.when(n == 6)
-        def _():
-            landed(5)
-            landed(7)
-            relay[1] = partial[d] + (inbox[5] + inbox[7])
-            sum_copy(relay.at[1], 4, 1, 0).start()
-
+    def project(n, proj):
+        d = turn(n)[1]
         chunk = basis2[:, pl.ds(pl.multiple_of(d * PIECE, PIECE), PIECE)]
         return proj + dot_nt(stacked(partial[d]), chunk)
 
-    proj = lax.fori_loop(0, 8, piece, jnp.zeros((2 * S, 2 * KS), f32))
+    proj = lax.fori_loop(0, 3, project, jnp.zeros((2 * S, 2 * KS), f32))
+    landed(6)
+    relay[0] = partial[col_peer(2)[0]] + inbox[6]
+    sum_copy(relay.at[0], 2, 0, 2).start()
+    proj = lax.fori_loop(3, 8, project, proj)
+    landed(5)
+    landed(7)
+    relay[1] = partial[col_peer(4)[0]] + (inbox[5] + inbox[7])
+    sum_copy(relay.at[1], 4, 1, 0).start()
     both = proj[:, :KS] + proj[:, KS:]
     stage_sib(1, fold(both))
     stage_row(1)
-    stage_end(0)
-    stage_col(1)
-
     for m in (1, 3, 2, 4):
         landed(m)
     total = partial[col] + (inbox[1] + inbox[3]) + (inbox[2] + inbox[4])
@@ -330,15 +338,27 @@
         arrival(product.at[k, rows], s3.at[h, 0], r3.at[h, k]).wait_recv()
 
     product[col] = total
-    for m in (4, 2, 1, 3):
+    own_product = stacked(total)
+    quads = dot_nt(own_product, own_product)
+    quads = quads[:, :S] + quads[:, S:]
+    stage_sib(2, jnp.concatenate([fold(quads), jnp.zeros((S, 128 - S), f32)], 1))
+    for m in (2, 1, 3):
         for h in range(2):
             spread(h, col, m, m)
+    stage_end(0)
+    stage_col(1)
+    stage_row(2)
+    for h in range(2):
+        spread(h, col, 4, 4)
+    stage_col(2)
 
     stage_end(1)
     first_proj = summed(1)
     basis_gram = jnp.concatenate([red_col[0, k] for k in range(8)], 0)
-    coeffs = 2.0 * first_proj - jnp.dot(
-        first_proj, basis_gram, precision=lax.Precision.HIGHEST, preferred_element_type=f32
+    coeffs = 2.0 * first_proj - exact(first_proj, basis_gram)
+    left_over = first_proj - exact(coeffs, basis_gram)
+    removed = exact_nt(
+        jnp.concatenate([first_proj, coeffs], 1), jnp.concatenate([coeffs, left_over], 1)
     )
     coeffs_out[...] = coeffs
     coeffs2 = wide(coeffs)
@@ -367,30 +387,25 @@
         for m in ms:
             foreseen[col_peer(m)[0]] = seen(col_peer(m)[0])
 
-    own_rest = keep(col, product[col] - seen(col))
-    quads = dot_nt(own_rest, own_rest)
-    quads = quads[:, :S] + quads[:, S:]
-    stage_sib(2, jnp.concatenate([fold(quads), jnp.zeros((S, 128 - S), f32)], 1))
-    for h in range(2):
-        k = col_peer(4)[0]
-        spread_wait(h, k)
-        spread(h, k, 5, 1)
-        spread(h, k, 6, 3)
-    stage_row(2)
-    for h in range(2):
-        k = col_peer(2)[0]
-        spread_wait(h, k)
-        spread(h, k, 7, 4)
-    foresee(1, 3, 4, 2)
-    stage_col(2)
-    foresee(5, 7, 6)
+    def hand_on(m, *next_peers):
+        k = col_peer(m)[0]
+        for h in range(2):
+            spread_wait(h, k)
+            for n, peer in next_peers:
+                spread(h, k, n, peer)
+
+    hand_on(4, (5, 1), (6, 3))
+    hand_on(2, (7, 4))
+    keep(col, product[col] - seen(col))
+    foresee(1, 3, 4, 2, 5, 7, 6)
     for m in (1, 3, 4, 2):
         remove(m)
     stage_end(2)
 
     lane = lax.broadcasted_iota(jnp.int32, (S, 128), 1)
     line = lax.broadcasted_iota(jnp.int32, (S, 128), 0)
-    work = jnp.where(lane == line + S, 1.0, summed(2))
+    gram = summed(2) - jnp.concatenate([removed, jnp.zeros((S, 128 - S), f32)], 1)
+    work = jnp.where(lane == line + S, 1.0, gram)
     factor = jnp.zeros((S, 128), f32)
     scale = jnp.zeros((S, 128), f32)
     for j in range(S):

time: 68.1 us -> 63 us (0.925)
  Pallas kernels: 67 us -> 61.4 us
    pallas_call x1, Pallas kernels: 63.3 us -> 57.7 us  [body(): pl.pallas_call(kernel, out_shape=(jax.ShapeDtypeStruct((8, 2 * S, PIECE),...]
where the time goes in v4:
time: 63 us; the launch traced here: 62.2 us
  Pallas kernels  61.4 us (97%)
  between operations  0.8 us (1%)
    pallas_call x1, Pallas kernels, body(): pl.pallas_call(kernel, out_shape=(jax.ShapeDtypeStruct((8, 2 * S, PIECE),...  57.7 us
    pallas_call x1, Pallas kernels, body(): pl.pallas_call(finish, out_shape=(jax.ShapeDtypeStruct((S, UNK), f32), ja...  3.76 us

profile of v4, /device:TPU:1, one launch (start us, length us, event | category | flops | bytes accessed | tf_op | source)
XLA Modules:
  0.0 62.2 jit_solution(14818860800972498011)
XLA Ops:
  0.6 57.7 %shard_map.76 = (bf16[8,32,2048]{2,1,0:T(8,128)(2,1)}, f32[16,128]{1,0:T(8,128)}, f32[16,16]{1,0:T(8,128)}, f32[16,128]{1,0:T(8,128)}) custom-call(s32[3,256]{1,0:T(4,128)} %bitcast.9, s32[1,256]{1,0:T(1,128)} %bitcast.10, f32[3,32,256,128]{3,2,1,0:T(8,128)} %bitcast.8, f32[16,16384]{1,0:T(8,128)} %vectors.1, f32[128,16384]{1,0:T(8,128)} %basis.1), custom_call_target="tpu_custom_call" | custom-call | tf_op jit(solution)/shard_map/pallas_call | solution.py:460
  58.3 3.8 %shard_map.77 = (f32[16,16384]{1,0:T(8,128)}, f32[16,128]{1,0:T(8,128)}, f32[16,16]{1,0:T(8,128)}) custom-call(bf16[8,32,2048]{2,1,0:T(8,128)(2,1)} %get-tuple-element.10.twice_in, f32[16,128]{1,0:T(8,128)} %get-tuple-element.11.coeffs_in, f32[16,16]{1,0:T(8,128)} %get-tuple-element.12.factor_in, f32[16,128]{1,0:T(8,128)} %get-tuple-element.13.inverse_in), custom_call_target="tpu_custom_call" | custom-call | tf_op jit(solution)/shard_map/pallas_call | solution.py:496

commit v5 on v4

--- a/solution.py
+++ b/solution.py
@@ -61,11 +61,11 @@
 
 
 def kernel(
-    columns, counts, blocks, vectors, basis,
+    columns_in, counts_in, blocks, vectors, basis,
     twice_out, coeffs_out, factor_out, inverse_out,
-    stage, weights, grid, expand, basis_stage, basis2, pieces, partial, inbox, relay, foreseen, product, twice,
+    columns, counts, small, stage, weights, grid, expand, basis_stage, basis2, pieces, partial, inbox, relay, foreseen, product, twice,
     red_src, red_sib, red_row, red_col,
-    load_sem, basis_sem, own_sem, out_sem,
+    index_sem, small_sem, load_sem, basis_sem, own_sem, out_sem,
     s1, r1, s2, r2, s3, r3, sib_s, sib_r, row_s, row_r, col_s, col_r,
 ):
     row = lax.axis_index("row")
@@ -83,6 +83,17 @@
         k = (yl + m // 4) % 2 * 4 + (z + m % 4) % 4
         return k, (row, k)
 
+    barrier = pltpu.get_barrier_semaphore()
+    peers = [sibling] + [row_peer(m)[1] for m in range(1, 8)] + [col_peer(m)[1] for m in range(1, 8)]
+    for peer in peers:
+        pl.semaphore_signal(barrier, inc=1, device_id=peer, device_id_type=MESH)
+
+    index_loads = [
+        pltpu.make_async_copy(columns_in, columns, index_sem.at[0]),
+        pltpu.make_async_copy(counts_in, counts, index_sem.at[1]),
+    ]
+    for load in index_loads:
+        load.start()
     own_loads = []
     for h in range(2):
         own_loads.append(
@@ -107,11 +118,6 @@
     basis_load(0).start()
     basis_load(1).start()
 
-    barrier = pltpu.get_barrier_semaphore()
-    peers = [sibling] + [row_peer(m)[1] for m in range(1, 8)] + [col_peer(m)[1] for m in range(1, 8)]
-    for peer in peers:
-        pl.semaphore_signal(barrier, inc=1, device_id=peer, device_id_type=MESH)
-
     cell = lax.broadcasted_iota(jnp.int32, (128, 512), 0)
     spot = lax.broadcasted_iota(jnp.int32, (128, 512), 1)
     expand[...] = jnp.where(
@@ -130,6 +136,8 @@
                 weights[band * BAND + i, 96 + 32 * s:128 + 32 * s, :] = lo
 
     pl.semaphore_wait(barrier, len(peers))
+    for load in index_loads:
+        load.wait()
 
     sends = []
 
@@ -236,22 +244,20 @@
     for h in range(2):
         for m in (4, 2, 1, 3):
             take(h, m)
+    prepare(row)
     for h in range(2):
         take_sibling(h, 0)
-    prepare(row)
     prepare(row + 1 - 2 * core)
     for m in (4, 2, 1, 3):
         prepare(row_peer(m)[0] * 2 + core)
-    for m in (5, 7, 6):
-        take(0, m)
-    for m in (4, 2, 1, 3):
         for h in range(2):
             take_sibling(h, m)
         prepare(row_peer(m)[0] * 2 + 1 - core)
+    for h in range(2):
+        for m in (5, 7, 6):
+            take(h, m)
     for m in (5, 7, 6):
-        take(1, m)
         prepare(row_peer(m)[0] * 2 + core)
-    for m in (5, 7, 6):
         for h in range(2):
             take_sibling(h, m)
         prepare(row_peer(m)[0] * 2 + 1 - core)
@@ -286,7 +292,7 @@
 
     def turn(n):
         m = n * 0
-        for place, peer in enumerate((6, 5, 7, 1, 3, 2, 4)):
+        for place, peer in enumerate((5, 7, 6, 1, 3, 2, 4)):
             m = jnp.where(n == place, peer, m)
         return m, (yl + m // 4) % 2 * 4 + (z + m % 4) % 4
 
@@ -300,11 +306,11 @@
                 jnp.where(low, even1, odd0), 64, 1
             )
 
-        @pl.when(n == 0)
+        @pl.when(n == 2)
         def _():
             sum_copy(partial.at[d], 6, 1, 0).start()
 
-        @pl.when((n >= 1) & (n < 5))
+        @pl.when((n < 5) & (n != 2))
         def _():
             sum_copy(partial.at[d], m, 0, m % 4).start()
 
@@ -313,15 +319,16 @@
         chunk = basis2[:, pl.ds(pl.multiple_of(d * PIECE, PIECE), PIECE)]
         return proj + dot_nt(stacked(partial[d]), chunk)
 
-    proj = lax.fori_loop(0, 3, project, jnp.zeros((2 * S, 2 * KS), f32))
-    landed(6)
-    relay[0] = partial[col_peer(2)[0]] + inbox[6]
-    sum_copy(relay.at[0], 2, 0, 2).start()
-    proj = lax.fori_loop(3, 8, project, proj)
+    proj = lax.fori_loop(0, 4, project, jnp.zeros((2 * S, 2 * KS), f32))
     landed(5)
     landed(7)
     relay[1] = partial[col_peer(4)[0]] + (inbox[5] + inbox[7])
     sum_copy(relay.at[1], 4, 1, 0).start()
+    proj = lax.fori_loop(4, 6, project, proj)
+    landed(6)
+    relay[0] = partial[col_peer(2)[0]] + inbox[6]
+    sum_copy(relay.at[0], 2, 0, 2).start()
+    proj = lax.fori_loop(6, 8, project, proj)
     both = proj[:, :KS] + proj[:, KS:]
     stage_sib(1, fold(both))
     stage_row(1)
@@ -338,31 +345,46 @@
         arrival(product.at[k, rows], s3.at[h, 0], r3.at[h, k]).wait_recv()
 
     product[col] = total
+    for m in (4, 2, 1, 3):
+        for h in range(2):
+            spread(h, col, m, m)
+    stage_end(0)
+    stage_col(1)
     own_product = stacked(total)
     quads = dot_nt(own_product, own_product)
     quads = quads[:, :S] + quads[:, S:]
     stage_sib(2, jnp.concatenate([fold(quads), jnp.zeros((S, 128 - S), f32)], 1))
-    for m in (2, 1, 3):
+    stage_row(2)
+
+    def hand_on(m, *next_peers):
+        k = col_peer(m)[0]
         for h in range(2):
-            spread(h, col, m, m)
-    stage_end(0)
-    stage_col(1)
-    stage_row(2)
-    for h in range(2):
-        spread(h, col, 4, 4)
+            spread_wait(h, k)
+            for n, peer in next_peers:
+                spread(h, k, n, peer)
+
+    hand_on(4, (5, 1), (6, 3))
+    hand_on(2, (7, 4))
     stage_col(2)
 
     stage_end(1)
     first_proj = summed(1)
     basis_gram = jnp.concatenate([red_col[0, k] for k in range(8)], 0)
+    writes = []
+
+    def small_copy(n, ref):
+        write = pltpu.make_async_copy(small.at[n], ref, small_sem.at[n])
+        write.start()
+        writes.append(write)
+
     coeffs = 2.0 * first_proj - exact(first_proj, basis_gram)
     left_over = first_proj - exact(coeffs, basis_gram)
     removed = exact_nt(
         jnp.concatenate([first_proj, coeffs], 1), jnp.concatenate([coeffs, left_over], 1)
     )
-    coeffs_out[...] = coeffs
+    small[0] = coeffs
+    small_copy(0, coeffs_out)
     coeffs2 = wide(coeffs)
-    writes = []
 
     def seen(k):
         chunk = basis2[:, pl.ds(pl.multiple_of(k * PIECE, PIECE), PIECE)]
@@ -387,15 +409,6 @@
         for m in ms:
             foreseen[col_peer(m)[0]] = seen(col_peer(m)[0])
 
-    def hand_on(m, *next_peers):
-        k = col_peer(m)[0]
-        for h in range(2):
-            spread_wait(h, k)
-            for n, peer in next_peers:
-                spread(h, k, n, peer)
-
-    hand_on(4, (5, 1), (6, 3))
-    hand_on(2, (7, 4))
     keep(col, product[col] - seen(col))
     foresee(1, 3, 4, 2, 5, 7, 6)
     for m in (1, 3, 4, 2):
@@ -416,8 +429,10 @@
         scale = jnp.where(line == j, root, scale)
         ratio = jnp.where(line > j, column / pivot, 0.0)
         work = work - ratio * jnp.broadcast_to(work[j:j + 1, :], (S, 128))
-    factor_out[...] = factor[:, :S]
-    inverse_out[...] = work * scale
+    small[1] = factor
+    small[2] = work * scale
+    small_copy(1, factor_out)
+    small_copy(2, inverse_out)
 
     for m in (5, 7, 6):
         remove(m)
@@ -430,21 +445,32 @@
         write.wait()
 
 
-def finish(twice_in, coeffs_in, factor_in, inverse_in, out, coeffs_out, factor_out, twice, final, in_sem, out_sem, small_sem):
-    loads, writes = [], []
-    for k in range(8):
-        loads.append(pltpu.make_async_copy(twice_in.at[k], twice.at[k], in_sem.at[k]))
-    writes.append(pltpu.make_async_copy(coeffs_in, coeffs_out, small_sem.at[0]))
-    writes.append(pltpu.make_async_copy(factor_in, factor_out, small_sem.at[1]))
-    for copy in loads + writes:
+def finish(
+    twice_in, coeffs_in, factor_in, inverse_in, out, coeffs_out, factor_out,
+    twice, final, small, corner, in_sem, out_sem, small_sem,
+):
+    load_small = [
+        pltpu.make_async_copy(inverse_in, small.at[0], small_sem.at[0]),
+        pltpu.make_async_copy(factor_in, small.at[1], small_sem.at[1]),
+    ]
+    loads = [pltpu.make_async_copy(twice_in.at[k], twice.at[k], in_sem.at[k]) for k in range(8)]
+    writes = [pltpu.make_async_copy(coeffs_in, coeffs_out, small_sem.at[2])]
+    for copy in load_small + loads + writes:
         copy.start()
-    inverse2 = wide(inverse_in[...][:, S:2 * S])
+    load_small[0].wait()
+    inverse2 = wide(small[0][:, S:2 * S])
     for k in range(8):
         loads[k].wait()
         final[k] = fold(dot(inverse2, twice[k]))
         write = pltpu.make_async_copy(final.at[k], out.at[:, pl.ds(k * PIECE, PIECE)], out_sem.at[k])
         write.start()
         writes.append(write)
+        if k == 0:
+            load_small[1].wait()
+            corner[...] = small[1][:, :S]
+            write = pltpu.make_async_copy(corner, factor_out, small_sem.at[3])
+            write.start()
+            writes.append(write)
     for write in writes:
         write.wait()
 
@@ -455,19 +481,20 @@
     D = pltpu.SemaphoreType.DMA
     V = pltpu.VMEM
     any_space = pl.BlockSpec(memory_space=pl.ANY)
-    smem = pl.BlockSpec(memory_space=pltpu.SMEM)
-    vmem = pl.BlockSpec(memory_space=pltpu.VMEM)
     twice, coeffs, factor, inverse = pl.pallas_call(
         kernel,
         out_shape=(
             jax.ShapeDtypeStruct((8, 2 * S, PIECE), bf16),
             jax.ShapeDtypeStruct((S, KS), f32),
-            jax.ShapeDtypeStruct((S, S), f32),
+            jax.ShapeDtypeStruct((S, 128), f32),
             jax.ShapeDtypeStruct((S, 128), f32),
         ),
-        in_specs=[smem, smem, any_space, any_space, any_space],
-        out_specs=(any_space, vmem, vmem, vmem),
+        in_specs=[any_space] * 5,
+        out_specs=(any_space,) * 4,
         scratch_shapes=[
+            pltpu.SMEM((SLOT, ROWS), jnp.int32),
+            pltpu.SMEM((1, ROWS), jnp.int32),
+            V((3, S, 128), f32),
             V((SLOT, ROWS // BAND, 32 * BAND, 128), f32),
             V((ROWS, 192, 128), bf16),
             V((ZERO_BLOCK + 1, 64, 128), bf16),
@@ -485,7 +512,7 @@
             V((3, S, 128), f32),
             V((3, 8, S, 128), f32),
             V((3, 8, S, 128), f32),
-            D((SLOT,)), D((2,)), D((2,)), D((8,)),
+            D((2,)), D((3,)), D((SLOT,)), D((2,)), D((2,)), D((8,)),
             D((2, 18)), D((2, 16)), D((8,)), D((8,)), D((2, 8)), D((2, 8)),
             D((3,)), D((3,)), D((3, 8)), D((3, 8)), D((3, 8)), D((3, 8)),
         ],
@@ -500,9 +527,12 @@
             jax.ShapeDtypeStruct((S, KS), f32),
             jax.ShapeDtypeStruct((S, S), f32),
         ),
-        in_specs=[any_space, any_space, any_space, vmem],
+        in_specs=[any_space] * 4,
         out_specs=(any_space, any_space, any_space),
-        scratch_shapes=[V((8, 2 * S, PIECE), bf16), V((8, S, PIECE), f32), D((8,)), D((8,)), D((2,))],
+        scratch_shapes=[
+            V((8, 2 * S, PIECE), bf16), V((8, S, PIECE), f32), V((2, S, 128), f32), V((S, S), f32),
+            D((8,)), D((8,)), D((4,)),
+        ],
         compiler_params=pltpu.CompilerParams(vmem_limit_bytes=62 << 20),
     )(twice, coeffs, factor, inverse)
     return new_block, coeffs.T, factor

time: 63 us -> 59.8 us (0.949)
  Pallas kernels: 61.4 us -> 58.8 us
    pallas_call x1, Pallas kernels: 57.7 us -> 55.6 us  [body(): pl.pallas_call(kernel, out_shape=(jax.ShapeDtypeStruct((8, 2 * S, PIECE),...]
where the time goes in v5:
time: 59.8 us; the launch traced here: 59.6 us
  Pallas kernels  58.8 us (98%)
  between operations  0.8 us (1%)
    pallas_call x1, Pallas kernels, body(): pl.pallas_call(kernel, out_shape=(jax.ShapeDtypeStruct((8, 2 * S, PIECE),...  55.6 us
    pallas_call x1, Pallas kernels, body(): pl.pallas_call(finish, out_shape=(jax.ShapeDtypeStruct((S, UNK), f32), ja...  3.28 us

profile of v5, /device:TPU:1, one launch (start us, length us, event | category | flops | bytes accessed | tf_op | source)
XLA Modules:
  0.0 59.6 jit_solution(14893677647398110093)
XLA Ops:
  0.6 55.6 %shard_map.76 = (bf16[8,32,2048]{2,1,0:T(8,128)(2,1)}, f32[16,128]{1,0:T(8,128)}, f32[16,128]{1,0:T(8,128)}, f32[16,128]{1,0:T(8,128)}) custom-call(s32[3,256]{1,0:T(4,128)} %bitcast.9, s32[1,256]{1,0:T(1,128)} %bitcast.10, f32[3,32,256,128]{3,2,1,0:T(8,128)} %bitcast.8, f32[16,16384]{1,0:T(8,128)} %vectors.1, f32[128,16384]{1,0:T(8,128)} %basis.1), custom_call_target="tpu_custom_call" | custom-call | tf_op jit(solution)/shard_map/pallas_call | solution.py:484
  56.2 3.3 %shard_map.77 = (f32[16,16384]{1,0:T(8,128)}, f32[16,128]{1,0:T(8,128)}, f32[16,16]{1,0:T(8,128)}) custom-call(bf16[8,32,2048]{2,1,0:T(8,128)(2,1)} %get-tuple-element.10.twice_in, f32[16,128]{1,0:T(8,128)} %get-tuple-element.11.coeffs_in, f32[16,128]{1,0:T(8,128)} %get-tuple-element.12.factor_in, f32[16,128]{1,0:T(8,128)} %get-tuple-element.13.inverse_in), custom_call_target="tpu_custom_call" | custom-call | tf_op jit(solution)/shard_map/pallas_call | solution.py:523

commit v6 on v5

--- a/solution.py
+++ b/solution.py
@@ -262,8 +262,6 @@
             take_sibling(h, m)
         prepare(row_peer(m)[0] * 2 + 1 - core)
 
-    stage_col(0)
-
     low = lax.broadcasted_iota(jnp.int32, (S, 128), 1) < 64
     group = lax.broadcasted_iota(jnp.int32, (64, 128), 1) // 32
 
@@ -331,6 +329,7 @@
     proj = lax.fori_loop(6, 8, project, proj)
     both = proj[:, :KS] + proj[:, KS:]
     stage_sib(1, fold(both))
+    stage_col(0)
     stage_row(1)
     for m in (1, 3, 2, 4):
         landed(m)

time: 59.8 us -> 60.3 us (level); the launches traced: 59.6 us -> 59.5 us
  no operation moved by 1% of the time
where the time goes in v6:
time: 60.3 us; the launch traced here: 59.5 us
  Pallas kernels  58.7 us (97%)
  between operations  0.8 us (1%)
    pallas_call x1, Pallas kernels, body(): pl.pallas_call(kernel, out_shape=(jax.ShapeDtypeStruct((8, 2 * S, PIECE),...  55.4 us
    pallas_call x1, Pallas kernels, body(): pl.pallas_call(finish, out_shape=(jax.ShapeDtypeStruct((S, UNK), f32), ja...  3.28 us

profile of v6, /device:TPU:1, one launch (start us, length us, event | category | flops | bytes accessed | tf_op | source)
XLA Modules:
  0.0 59.5 jit_solution(2514463233651223034)
XLA Ops:
  0.6 55.4 %shard_map.76 = (bf16[8,32,2048]{2,1,0:T(8,128)(2,1)}, f32[16,128]{1,0:T(8,128)}, f32[16,128]{1,0:T(8,128)}, f32[16,128]{1,0:T(8,128)}) custom-call(s32[3,256]{1,0:T(4,128)} %bitcast.9, s32[1,256]{1,0:T(1,128)} %bitcast.10, f32[3,32,256,128]{3,2,1,0:T(8,128)} %bitcast.8, f32[16,16384]{1,0:T(8,128)} %vectors.1, f32[128,16384]{1,0:T(8,128)} %basis.1), custom_call_target="tpu_custom_call" | custom-call | tf_op jit(solution)/shard_map/pallas_call | solution.py:483
  56.0 3.3 %shard_map.77 = (f32[16,16384]{1,0:T(8,128)}, f32[16,128]{1,0:T(8,128)}, f32[16,16]{1,0:T(8,128)}) custom-call(bf16[8,32,2048]{2,1,0:T(8,128)(2,1)} %get-tuple-element.10.twice_in, f32[16,128]{1,0:T(8,128)} %get-tuple-element.11.coeffs_in, f32[16,128]{1,0:T(8,128)} %get-tuple-element.12.factor_in, f32[16,128]{1,0:T(8,128)} %get-tuple-element.13.inverse_in), custom_call_target="tpu_custom_call" | custom-call | tf_op jit(solution)/shard_map/pallas_call | solution.py:522
